TPU v7x, 32 devices: a whole 2x2x4 slice. The times are simulated.
32 devices in a mesh: fsdp: 32 (over z, y, x, core).
Axes of the slice: x: 2, y: 2, z: 4, core: 2. Of those that a mesh axis runs over, the one named last changes fastest.
Arguments:
- inputs: bfloat16 [8192, 2048], P('fsdp'), may hold values from -6 to 6
- doc_ids: int32 [32, 256], P('fsdp'), may hold values from 0 to 63, never falling along the last dimension, each value on 1 to 128 neighbouring positions
- attn_gain: bfloat16 [2048], P('fsdp'), may hold values from 0.5 to 1.5
- attn_shift: bfloat16 [2048], P('fsdp'), may hold values from -1.1953125 to 1.1953125
- ffn_gain: bfloat16 [2048], P('fsdp'), may hold values from 0.5 to 1.5
- ffn_shift: bfloat16 [2048], P('fsdp'), may hold values from -1.1953125 to 1.1953125
- qkv_weight: bfloat16 [2048, 6144], P('fsdp'), may hold values from -0.125 to 0.125
- qkv_bias: bfloat16 [6144], P('fsdp'), may hold values from -1.1953125 to 1.1953125
- proj_weight: bfloat16 [2048, 2048], P('fsdp'), may hold values from -0.5 to 0.5
- proj_bias: bfloat16 [2048], P('fsdp'), may hold values from -1.1953125 to 1.1953125
- up_weight: bfloat16 [2048, 8192], P('fsdp'), may hold values from -0.125 to 0.125
- up_bias: bfloat16 [8192], P('fsdp'), may hold values from -1.1953125 to 1.1953125
- down_weight: bfloat16 [8192, 2048], P('fsdp'), may hold values from -0.09375 to 0.09375
- down_bias: bfloat16 [2048], P('fsdp'), may hold values from -1.1953125 to 1.1953125
- cotangent: bfloat16 [8192, 2048], P('fsdp'), may hold values from -6 to 6
Outputs:
- layer_out: float32 [8192, 2048], P('fsdp')
- grad_inputs: float32 [8192, 2048], P('fsdp')
- grad_attn_gain: float32 [2048], P('fsdp')
- grad_attn_shift: float32 [2048], P('fsdp')
- grad_ffn_gain: float32 [2048], P('fsdp')
- grad_ffn_shift: float32 [2048], P('fsdp')
- grad_qkv_weight: float32 [2048, 6144], P('fsdp')
- grad_qkv_bias: float32 [6144], P('fsdp')
- grad_proj_weight: float32 [2048, 2048], P('fsdp')
- grad_proj_bias: float32 [2048], P('fsdp')
- grad_up_weight: float32 [2048, 8192], P('fsdp')
- grad_up_bias: float32 [8192], P('fsdp')
- grad_down_weight: float32 [8192, 2048], P('fsdp')
- grad_down_bias: float32 [2048], P('fsdp')
All inputs are finite; a program needn't handle non-finite values.
Results may differ from a plain program's by a relative error of at most 0.0069.
Values may be sent and summed in bfloat16 or wider, within the bound.
No kernel may reach another device: no remote copies, remote signals or barrier semaphores. Data moves between devices by JAX's collectives and lax.ppermute only.
A program may use at most 704 MiB of HBM per device.

v0:
```python
import jax
import jax.numpy as jnp
from jax import lax
from jax.sharding import PartitionSpec as P

HEADS = 8
HEAD = 256
ROT = 64


EPS = 1e-05
MASKED = -1e30


def norm(value, gain, shift):
    center = value - jnp.mean(value, axis=-1, keepdims=True)
    spread = jnp.mean(center * center, axis=-1, keepdims=True)
    return center * lax.rsqrt(spread + EPS) * gain + shift


def rotate(value, position):
    half = ROT // 2
    freq = 10000.0 ** (-2.0 * jnp.arange(half, dtype=jnp.float32) / ROT)
    angle = position.astype(jnp.float32)[:, None] * freq[None, :]
    cosine = jnp.cos(angle)[:, None, :]
    sine = jnp.sin(angle)[:, None, :]
    front = value[..., :half]
    back = value[..., half:ROT]
    return jnp.concatenate(
        [front * cosine - back * sine, back * cosine + front * sine, value[..., ROT:]], axis=-1
    )


def layout(docs):
    index = jnp.arange(docs.shape[0], dtype=jnp.int32)
    same = docs[:, None] == docs[None, :]
    before = index[None, :] < index[:, None]
    position = jnp.sum((same & before).astype(jnp.int32), axis=1)
    allowed = same & (index[None, :] <= index[:, None])
    return (position, allowed)


def times_rows(left, right):
    return jnp.einsum("tc,nc->tn", left, right, preferred_element_type=jnp.float32)


def local(
    inputs,
    doc_ids,
    attn_gain,
    attn_shift,
    ffn_gain,
    ffn_shift,
    qkv_weight,
    qkv_bias,
    proj_weight,
    proj_bias,
    up_weight,
    up_bias,
    down_weight,
    down_bias,
    cotangent,
):
    value = inputs.astype(jnp.float32)
    count = value.shape[0]
    width = value.shape[1]
    ratio = down_weight.shape[0] // proj_weight.shape[0]
    down_fold = down_weight.reshape(proj_weight.shape[0], -1)
    position, allowed = layout(doc_ids[0])
    vectors = (
        lax.all_gather(attn_gain, "fsdp", axis=0, tiled=True),
        lax.all_gather(attn_shift, "fsdp", axis=0, tiled=True),
        lax.all_gather(ffn_gain, "fsdp", axis=0, tiled=True),
        lax.all_gather(ffn_shift, "fsdp", axis=0, tiled=True),
        lax.all_gather(qkv_bias, "fsdp", axis=0, tiled=True),
        lax.all_gather(proj_bias, "fsdp", axis=0, tiled=True),
        lax.all_gather(up_bias, "fsdp", axis=0, tiled=True),
        lax.all_gather(down_bias, "fsdp", axis=0, tiled=True),
    )
    a_gain, a_shift, f_gain, f_shift, b_qkv, b_proj, b_up, b_down = [
        v.astype(jnp.float32) for v in vectors
    ]
    first = norm(value, a_gain, a_shift).astype(jnp.bfloat16)
    second = norm(value, f_gain, f_shift).astype(jnp.bfloat16)
    pieces = (
        lax.all_gather(qkv_weight, "fsdp", axis=0, tiled=True),
        lax.all_gather(up_weight, "fsdp", axis=0, tiled=True),
    )
    left = first
    right = second
    qkv = jnp.dot(left, pieces[0], preferred_element_type=jnp.float32)
    up_sum = jnp.dot(right, pieces[1], preferred_element_type=jnp.float32)
    qkv = qkv + b_qkv
    up = up_sum + b_up
    query = qkv[:, :width].reshape(count, HEADS, HEAD)
    keys = qkv[:, width : 2 * width].reshape(count, HEADS, HEAD)
    values = qkv[:, 2 * width :].reshape(count, HEADS, HEAD)
    rot_query = rotate(query, position).astype(jnp.bfloat16)
    rot_keys = rotate(keys, position).astype(jnp.bfloat16)
    low_values = values.astype(jnp.bfloat16)
    scale = HEAD ** (-0.5)
    raw = jnp.einsum("thd,shd->hts", rot_query, rot_keys, preferred_element_type=jnp.float32)
    scores = jnp.where(allowed[None], raw * scale, MASKED)
    top = jnp.max(scores, axis=-1, keepdims=True)
    expo = jnp.exp(scores - top)
    probs = expo / jnp.sum(expo, axis=-1, keepdims=True)
    low_probs = probs.astype(jnp.bfloat16)
    mixed = jnp.einsum("hts,shd->thd", low_probs, low_values, preferred_element_type=jnp.float32)
    mixed = mixed.reshape(count, width).astype(jnp.bfloat16)
    act = jax.nn.gelu(up, approximate=False).astype(jnp.bfloat16)
    pieces = (
        lax.all_gather(proj_weight, "fsdp", axis=0, tiled=True),
        lax.all_gather(down_fold, "fsdp", axis=0, tiled=True),
    )
    rows = pieces[0].shape[0]
    left = mixed
    right = act
    term = jnp.dot(left, pieces[0], preferred_element_type=jnp.float32)
    branches = term + jnp.dot(
        right, pieces[1].reshape(rows * ratio, -1), preferred_element_type=jnp.float32
    )
    layer_out = value + branches + b_proj + b_down
    grad32 = cotangent.astype(jnp.float32)
    pieces = (
        lax.all_gather(proj_weight, "fsdp", axis=0, tiled=True),
        lax.all_gather(down_fold, "fsdp", axis=0, tiled=True),
    )
    rows = pieces[0].shape[0]
    left = times_rows(cotangent, pieces[0])
    right = times_rows(cotangent, pieces[1].reshape(rows * ratio, -1))
    d_mixed = left
    d_act = right
    d_mixed = d_mixed.astype(jnp.bfloat16).reshape(count, HEADS, HEAD)
    gelu_out, gelu_pull = jax.vjp(lambda u: jax.nn.gelu(u, approximate=False), up)
    d_up = gelu_pull(d_act)[0].astype(jnp.bfloat16)
    d_prob = jnp.einsum("thd,shd->hts", d_mixed, low_values, preferred_element_type=jnp.float32)
    d_score = probs * (d_prob - jnp.sum(probs * d_prob, axis=-1, keepdims=True))
    d_raw = (d_score * scale).astype(jnp.bfloat16)
    d_query = jnp.einsum("hts,shd->thd", d_raw, rot_keys, preferred_element_type=jnp.float32)
    d_keys = jnp.einsum("hts,thd->shd", d_raw, rot_query, preferred_element_type=jnp.float32)
    d_values = jnp.einsum("hts,thd->shd", low_probs, d_mixed, preferred_element_type=jnp.float32)
    turned, turn_pull = jax.vjp(lambda a: rotate(a, position), query)
    back_query = turn_pull(d_query)[0]
    back_keys = turn_pull(d_keys)[0]
    d_qkv = jnp.concatenate(
        [
            back_query.reshape(count, width),
            back_keys.reshape(count, width),
            d_values.reshape(count, width),
        ],
        axis=1,
    ).astype(jnp.bfloat16)
    pieces = (
        lax.all_gather(qkv_weight, "fsdp", axis=0, tiled=True),
        lax.all_gather(up_weight, "fsdp", axis=0, tiled=True),
    )
    left = times_rows(d_qkv, pieces[0])
    right = times_rows(d_up, pieces[1])
    d_first = left
    d_second = right
    normed, first_pull = jax.vjp(norm, value, a_gain, a_shift)
    dx_first, dg_first, ds_first = first_pull(d_first)
    normed, second_pull = jax.vjp(norm, value, f_gain, f_shift)
    dx_second, dg_second, ds_second = second_pull(d_second)
    grad_inputs = grad32 + dx_first + dx_second
    left = mixed
    right = act
    part_proj = jnp.einsum("tn,td->nd", left, cotangent, preferred_element_type=jnp.float32)
    part_down = jnp.einsum(
        "tn,td->nd", right, cotangent, preferred_element_type=jnp.float32
    ).reshape(proj_weight.shape[0] * lax.axis_size("fsdp"), -1)
    out_grads = lax.psum_scatter(
        jnp.concatenate([part_proj, part_down], axis=1), "fsdp", scatter_dimension=0, tiled=True
    )
    left = first
    right = second
    part_qkv = jnp.einsum("tn,tc->nc", left, d_qkv, preferred_element_type=jnp.float32)
    part_up = jnp.einsum("tn,tc->nc", right, d_up, preferred_element_type=jnp.float32)
    in_grads = lax.psum_scatter(
        jnp.concatenate([part_qkv, part_up], axis=1), "fsdp", scatter_dimension=0, tiled=True
    )
    column_qkv = jnp.sum(d_qkv.astype(jnp.float32), axis=0)
    column_up = jnp.sum(d_up.astype(jnp.float32), axis=0)
    column_out = jnp.sum(grad32, axis=0)
    sums = (
        lax.psum_scatter(dg_first, "fsdp", scatter_dimension=0, tiled=True),
        lax.psum_scatter(ds_first, "fsdp", scatter_dimension=0, tiled=True),
        lax.psum_scatter(dg_second, "fsdp", scatter_dimension=0, tiled=True),
        lax.psum_scatter(ds_second, "fsdp", scatter_dimension=0, tiled=True),
        lax.psum_scatter(column_qkv, "fsdp", scatter_dimension=0, tiled=True),
        lax.psum_scatter(column_up, "fsdp", scatter_dimension=0, tiled=True),
        lax.psum_scatter(column_out, "fsdp", scatter_dimension=0, tiled=True),
    )
    grad_qkv_weight = in_grads[:, : 3 * width]
    grad_up_weight = in_grads[:, 3 * width :]
    grad_proj_weight = out_grads[:, :width]
    grad_down_weight = out_grads[:, width:].reshape(-1, width)
    return (
        layer_out,
        grad_inputs,
        sums[0],
        sums[1],
        sums[2],
        sums[3],
        grad_qkv_weight,
        sums[4],
        grad_proj_weight,
        sums[6],
        grad_up_weight,
        sums[5],
        grad_down_weight,
        sums[6],
    )


def solution(mesh):
    return jax.shard_map(
        local,
        mesh=mesh,
        in_specs=(
            P("fsdp", None),
            P("fsdp", None),
            P("fsdp"),
            P("fsdp"),
            P("fsdp"),
            P("fsdp"),
            P("fsdp", None),
            P("fsdp"),
            P("fsdp", None),
            P("fsdp"),
            P("fsdp", None),
            P("fsdp"),
            P("fsdp", None),
            P("fsdp"),
            P("fsdp", None),
        ),
        out_specs=(
            P("fsdp", None),
            P("fsdp", None),
            P("fsdp"),
            P("fsdp"),
            P("fsdp"),
            P("fsdp"),
            P("fsdp", None),
            P("fsdp"),
            P("fsdp", None),
            P("fsdp"),
            P("fsdp", None),
            P("fsdp"),
            P("fsdp", None),
            P("fsdp"),
        ),
        check_vma=False,
    )
```

profile of v0, /device:TPU:0, one launch (start us, length us, event | category | flops | bytes accessed | tf_op | source)
XLA Modules:
  0.0 3414.6 jit_solution(100484155062352815)
XLA Ops:
  14.2 43.6 %all-reduce.22 = (bf16[6144]{0:T(1024)(128)(2,1)S(1)}, bf16[2048]{0:T(1024)(128)(2,1)S(1)}, bf16[2048]{0:T(1024)(128)(2,1)S(1)}, bf16[2048]{0:T(1024)(128)(2,1)S...) all-reduce(bf16[6144]{0:T(1024)(128)(2,1)S(1)} %dynamic-update-slic, ...), channel_id=1, replica_groups=mesh['fsdp'=32] {'fsdp'}, use_global_device_ids=true, to_apply=%add.8 | all-reduce | flops 18432 | bytes 73728
  58.4 40.0 %all-gather = bf16[32,1,256]{2,1,0:T(2,128)(2,1)S(1)} all-gather(bf16[1,1,256]{2,1,0:T(2,128)(2,1)S(1)} %reshape.245), channel_id=1, replica_groups=mesh['fsdp'=32] {'fsdp'}, dimensions={0}, use_global_device_ids=true | all-gather | bytes 16896 | tf_op jit(solution)/shard_map/all_gather | solution.py:77
  99.9 7.4 convolution_convert_fusion
  108.8 138.7 %all-gather.6.cloned.1.call-done = bf16[2048,6144]{1,0:T(8,128)(2,1)} async-done(((bf16[64,6144]{1,0:T(8,128)(2,1)}), bf16[2048,6144]{1,0:T(8,128)(2,1)}) %all-gather.6.cloned.1.call-update) | async-done | bytes 25165840 | tf_op jit(solution)/shard_map/all_gather | solution.py:86
  247.5 12.0 convolution_add_fusion.1
  269.5 5.3 fusion.82
  274.8 6.9 fusion.43
  281.7 3.5 split.27
  285.2 6.7 fusion.40
  291.9 3.7 split.24
  301.3 4.7 add_convert_fusion.2
  312.4 19.8 fusion.70
  332.2 111.2 %all-gather.12.cloned.1.call-done = bf16[2048,8192]{1,0:T(8,128)(2,1)} async-done(((bf16[64,8192]{1,0:T(8,128)(2,1)}), bf16[2048,8192]{1,0:T(8,128)(2,1)}) %all-gather.12.cloned.1.call-update) | async-done | bytes 33554448 | tf_op jit(solution)/shard_map/all_gather | solution.py:113
  443.4 55.4 %reshape.224 = bf16[8192,2048]{1,0:T(8,128)(2,1)} reshape(bf16[2048,8192]{1,0:T(8,128)(2,1)} %all-gather.12.cloned.1.call-done) | data formatting | bytes 67108864 | tf_op jit(solution)/shard_map/reshape | solution.py:120
  498.8 140.3 %all-gather.10.cloned.1.call-done = bf16[2048,8192]{1,0:T(8,128)(2,1)} async-done(((bf16[64,8192]{1,0:T(8,128)(2,1)}), bf16[2048,8192]{1,0:T(8,128)(2,1)}) %all-gather.10.cloned.1.call-update) | async-done | bytes 33554448 | tf_op jit(solution)/shard_map/all_gather | solution.py:87
  639.1 17.2 convolution_add_fusion
  656.3 34.5 %convert_reduce_fusion = (f32[8192]{0:T(1024)}, bf16[256,8192]{1,0:T(8,128)(2,1)}, f32[256,8192]{1,0:T(8,128)}) fusion(f32[256,8192]{1,0:T(8,128)} %convolution_add_fusion, bf16[256,2048]{1,0:T(8,128)(2,1)S(1)} %copy-done.4, bf16[8192,2048]{1,0:T(8,128)(2,1)} %reshape.224), kind=kOutput, calls=%fused_computation.7 | convolution fusion | flops 8745115648 | bytes 55607296 | tf_op jit(solution)/shard_map/tc,nc->tn/dot_general | solution.py:44
  690.8 25.4 fusion.67
  716.2 17.0 fusion.84
  733.3 14.5 fusion.77
  747.8 4.6 fusion.26
  756.0 77.1 %pad_maximum_fusion = f32[2048,14336]{1,0:T(8,128)} fusion(f32[2048,8192]{1,0:T(8,128)} %fusion.67, f32[2048,6144]{1,0:T(8,128)} %fusion.70), kind=kLoop, calls=%fused_computation.2 | loop fusion | flops 29360128 | bytes 234881024 | tf_op jit(solution)/shard_map/concatenate | solution.py:180
  836.5 8.1 fusion.85
  844.5 7.2 multiply_convert_fusion
  853.7 23.4 fusion.86
  877.1 79.3 %reshape.229 = f32[2048,8192]{1,0:T(8,128)} reshape(f32[8192,2048]{1,0:T(8,128)} %fusion.86) | data formatting | bytes 134217728 | tf_op jit(solution)/shard_map/reshape | solution.py:171
  956.5 55.9 %pad_maximum_fusion.1 = f32[2048,10240]{1,0:T(8,128)} fusion(f32[2048,8192]{1,0:T(8,128)} %reshape.229, f32[2048,2048]{1,0:T(8,128)} %fusion.85), kind=kLoop, calls=%fused_computation.3 | loop fusion | flops 20971520 | bytes 167772160 | tf_op jit(solution)/shard_map/concatenate | solution.py:173
  1013.1 7.3 fusion.83
  1020.3 18.9 fusion.19
  1047.6 1475.6 %all-reduce.26.cloned.1.call-done = f32[2048,14336]{1,0:T(8,128)} async-done(((f32[2048,14336]{1,0:T(8,128)}), f32[2048,14336]{1,0:T(8,128)}) %all-reduce.26.cloned.1.call-update) | async-done | bytes 117440528
  2523.2 3.5 dynamic-slice.9
  2529.4 872.3 %reduce-scatter.2.cloned.1.call-done = f32[64,10240]{1,0:T(8,128)} async-done(((f32[2048,10240]{1,0:T(8,128)}), f32[64,10240]{1,0:T(8,128)}) %reduce-scatter.2.cloned.1.call-update) | async-done | bytes 2621456 | tf_op jit(solution)/shard_map/reduce_scatter | solution.py:172
  (160 shorter events, 58.4 us)
Async XLA Ops:
  7.2 92.7 %all-gather.8.cloned.1.call-start = ((), (), s32[]{:S(2)}) async-start(), calls=%async_computation.2 | async-start | bytes 8650752 | tf_op jit(solution)/shard_map/all_gather | solution.py:112
  7.9 239.6 %all-gather.6.cloned.1.call-start = ((), (), s32[]{:S(2)}) async-start(), calls=%async_computation.1 | async-start | bytes 25952256 | tf_op jit(solution)/shard_map/all_gather | solution.py:86
  8.7 3.7 copy-start.26
  8.7 3.7 copy-start.27
  8.7 4.0 copy-start.28
  8.7 4.2 copy-start.29
  8.7 4.5 copy-start.30
  8.7 4.7 copy-start.31
  8.7 4.9 copy-start.32
  8.7 5.2 copy-start.33
  8.8 89.8 %copy-start = (bf16[256,2048]{1,0:T(8,128)(2,1)S(1)}, bf16[256,2048]{1,0:T(8,128)(2,1)}, u32[]{:S(2)}) copy-start(bf16[256,2048]{1,0:T(8,128)(2,1)} %param.15) | copy-start | bytes 3145732
  8.8 434.6 %all-gather.12.cloned.1.call-start = ((), (), s32[]{:S(2)}) async-start(), calls=%async_computation.4 | async-start | bytes 34603008 | tf_op jit(solution)/shard_map/all_gather | solution.py:113
  11.6 88.3 %copy-start.4 = (bf16[256,2048]{1,0:T(8,128)(2,1)S(1)}, bf16[256,2048]{1,0:T(8,128)(2,1)}, u32[]{:S(2)}) copy-start(bf16[256,2048]{1,0:T(8,128)(2,1)} %param.29) | copy-start | bytes 3145732
  11.6 627.5 %all-gather.10.cloned.1.call-start = ((), (), s32[]{:S(2)}) async-start(), calls=%async_computation.3 | async-start | bytes 34603008 | tf_op jit(solution)/shard_map/all_gather | solution.py:87
  12.2 1027.0 %all-reduce.28.cloned.1.call-start = ((), (), s32[]{:S(2)}) async-start(), calls=%async_computation.7 | async-start | bytes 196608
  57.8 254.6 %copy-start.19 = (f32[2048]{0:T(1024)}, f32[2048]{0:T(1024)S(1)}, u32[]{:S(2)}) copy-start(f32[2048]{0:T(1024)S(1)} %convert_element_type.86) | copy-start | bytes 24580
  108.8 156.1 %copy-start.17 = (bf16[256,2048]{0,1:T(8,128)(2,1)}, bf16[256,2048]{0,1:T(8,128)(2,1)S(1)}, u32[]{:S(2)}) copy-start(bf16[256,2048]{0,1:T(8,128)(2,1)S(1)} %copy.99) | copy-start | bytes 3145732
  259.7 5.2 copy-start.15
  274.8 33.4 copy-start.35
  291.9 3.7 copy-start.13
  301.3 11.1 copy-start.5
  716.2 17.0 copy-start.6
  716.2 17.0 copy-start.8
  716.2 17.0 copy-start.20
  733.3 14.5 copy-start.23
  747.8 4.7 copy-start.9
  747.8 4.6 copy-start.10
  756.0 1767.3 %all-reduce.26.cloned.1.call-start = ((), (), s32[]{:S(2)}) async-start(), calls=%async_computation.6 | async-start | bytes 234881024
  833.2 2568.5 %reduce-scatter.2.cloned.1.call-start = ((), (), s32[]{:S(2)}) async-start(), calls=%async_computation.5 | async-start | bytes 86507520 | tf_op jit(solution)/shard_map/reduce_scatter | solution.py:172
  1013.1 7.3 copy-start.1
  1013.1 7.3 copy-start.3
  1041.2 2365.5 %copy-start.34 = (f32[64]{0:T(128)}, f32[64]{0:T(128)S(1)}, u32[]{:S(2)}) copy-start(f32[64]{0:T(128)S(1)} %dynamic-slice.6) | copy-start | bytes 772
  (13 other events, 23.6 us)
Sparse Core Ops, SparseCore 0:
  10.9 80.4 all-gather.7
  94.2 153.2 all-gather.5
  250.4 192.9 all-gather.11
  446.1 192.9 all-gather.9
  756.1 122.0 all-reduce.27
  885.6 1637.5 all-reduce.25
  2525.6 876.0 reduce-scatter.1
where the time goes:
time: 3430 us; the launch traced here: 3410 us
  waiting for transfers between devices  2740 us (80%)
  matrix products  231 us (7%)
  local copies, waits for them, and re-layouts  182 us (5%)
  other arithmetic  163 us (5%)
  blocking collectives  83.7 us (2%)
    unnamed x9, waiting for transfers between devices  1480 us
    reduce_scatter x1, waiting for transfers between devices, local(): lax.psum_scatter(jnp.concatenate([part_proj, part_down], axis=1), 'fsdp',...  872 us
    all_gather x1, waiting for transfers between devices, local(): lax.all_gather(up_weight, 'fsdp', axis=0, tiled=True)  140 us
    all_gather x1, waiting for transfers between devices, local(): lax.all_gather(qkv_weight, 'fsdp', axis=0, tiled=True)  139 us
    all_gather x1, waiting for transfers between devices, local(): lax.all_gather(down_fold, 'fsdp', axis=0, tiled=True)  111 us
    reshape x1, local copies, waits for them, and re-layouts, local(): part_down = jnp.einsum('tn,td->nd', right, cotangent, preferred_element_t...  79.3 us
    concatenate x1, other arithmetic, local(): jnp.concatenate([part_qkv, part_up], axis=1)  77.1 us
    dot_general x4, matrix products, times_rows(): jnp.einsum('tc,nc->tn', left, right, preferred_element_type=jnp.float32)  73.4 us
  transfers between devices with their start and end apart: 7, of which 5 were waited for; matrix products, arithmetic and copies ran while one was open for 13% of the time, Pallas kernels for 0%

commit v1 on v0

v1 whole, which is shorter than its diff:
```python
import functools

import jax
import jax.numpy as jnp
from jax import lax
from jax.experimental import pallas as pl
from jax.experimental.pallas import tpu as pltpu
from jax.sharding import PartitionSpec as P

HEADS = 8
HEAD = 256
ROT = 64
EPS = 1e-05
MASKED = -1e30
AXIS = "fsdp"
BF16 = jnp.bfloat16
F32 = jnp.float32

SPLIT_BITS = {32: (3, 2, 0), 128: (3, 1, 0)}


def attention_kernel(qkv_ref, turn_ref, docs_row_ref, docs_col_ref, d_mixed_ref, mixed_ref, d_qkv_ref, column_ref):
    half = ROT // 2
    cosine = turn_ref[0]
    sine = turn_ref[1]
    lanes = cosine.shape[1]
    lane = lax.broadcasted_iota(jnp.int32, cosine.shape, 1)

    def swap(v):
        return jnp.where(lane < half, pltpu.roll(v, lanes - half, 1), pltpu.roll(v, half, 1))

    def turn(v, sign):
        front = v[:, :lanes]
        front = front * cosine + sign * (swap(front) * sine)
        return jnp.concatenate([front, v[:, lanes:]], axis=1)

    rq = turn(qkv_ref[:, :HEAD], 1.0).astype(BF16)
    rk = turn(qkv_ref[:, HEAD : 2 * HEAD], 1.0).astype(BF16)
    rv = qkv_ref[:, 2 * HEAD :].astype(BF16)
    count = rq.shape[0]
    here = lax.broadcasted_iota(jnp.int32, (count, count), 0)
    there = lax.broadcasted_iota(jnp.int32, (count, count), 1)
    allowed = (docs_row_ref[0] == docs_col_ref[0]) & (there <= here)
    scale = HEAD ** (-0.5)
    rows = (((1,), (1,)), ((), ()))
    firsts = (((0,), (0,)), ((), ()))
    raw = lax.dot_general(rq, rk, rows, preferred_element_type=F32)
    scores = jnp.where(allowed, raw * scale, MASKED)
    expo = jnp.exp(scores - jnp.max(scores, axis=1, keepdims=True))
    probs = expo / jnp.sum(expo, axis=1, keepdims=True)
    weights = probs.astype(BF16)
    mixed_ref[...] = jnp.dot(weights, rv, preferred_element_type=F32).astype(BF16)
    d_mixed = d_mixed_ref[...]
    d_prob = lax.dot_general(d_mixed, rv, rows, preferred_element_type=F32)
    d_score = probs * (d_prob - jnp.sum(probs * d_prob, axis=1, keepdims=True))
    d_raw = (d_score * scale).astype(BF16)
    d_rq = jnp.dot(d_raw, rk, preferred_element_type=F32)
    d_rk = lax.dot_general(d_raw, rq, firsts, preferred_element_type=F32)
    d_rv = lax.dot_general(weights, d_mixed, firsts, preferred_element_type=F32)
    d_qkv = jnp.concatenate([turn(d_rq, -1.0), turn(d_rk, -1.0), d_rv], axis=1).astype(BF16)
    d_qkv_ref[...] = d_qkv

    @pl.when(pl.program_id(0) == 0)
    def _():
        column_ref[...] = jnp.zeros_like(column_ref)

    column_ref[...] += jnp.sum(d_qkv.astype(F32), axis=0, keepdims=True)


def attention(qkv, cosine, sine, docs, d_mixed):
    rows, count = docs.shape
    turns = jnp.stack([cosine, sine])
    lanes = turns.shape[2]
    return pl.pallas_call(
        attention_kernel,
        grid=(rows,),
        in_specs=[
            pl.BlockSpec((count, 3 * HEAD), lambda i: (i, 0)),
            pl.BlockSpec((2, count, lanes), lambda i: (0, i, 0)),
            pl.BlockSpec((1, 1, count), lambda i: (i, 0, 0)),
            pl.BlockSpec((1, count, 1), lambda i: (i, 0, 0)),
            pl.BlockSpec((count, HEAD), lambda i: (i, 0)),
        ],
        out_specs=[
            pl.BlockSpec((count, HEAD), lambda i: (i, 0)),
            pl.BlockSpec((count, 3 * HEAD), lambda i: (i, 0)),
            pl.BlockSpec((1, 3 * HEAD), lambda i: (0, 0)),
        ],
        out_shape=[
            jax.ShapeDtypeStruct((rows * count, HEAD), BF16),
            jax.ShapeDtypeStruct((rows * count, 3 * HEAD), BF16),
            jax.ShapeDtypeStruct((1, 3 * HEAD), F32),
        ],
        compiler_params=pltpu.CompilerParams(vmem_limit_bytes=32 * 1024 * 1024),
        cost_estimate=pl.CostEstimate(
            flops=16 * rows * count * count * HEAD, bytes_accessed=20 * rows * count * HEAD, transcendentals=rows * count * count
        ),
    )(qkv, turns, docs[:, None, :], docs[:, :, None], d_mixed)


def times_rows(left, right):
    return jnp.einsum("tc,nc->tn", left, right, preferred_element_type=F32)


def times_tokens(left, right):
    return jnp.einsum("tn,td->nd", left, right, preferred_element_type=F32)


class Layout:
    def __init__(self, count):
        self.count = count
        self.bits = count.bit_length() - 1
        self.h_bits = SPLIT_BITS.get(count, (2, 1, 0))
        self.t_bits = tuple(b for b in range(self.bits - 1, -1, -1) if b not in self.h_bits)
        head_bits = tuple(range(self.bits - 1, self.bits - 4, -1))
        self.swap = {b: b for b in range(self.bits)}
        for a, b in zip([a for a in head_bits if a not in self.h_bits], [b for b in self.h_bits if b not in head_bits]):
            self.swap[a], self.swap[b] = b, a
        self.groups = []
        for t in range(1 << len(self.t_bits)):
            base = sum(((t >> (len(self.t_bits) - 1 - i)) & 1) << b for i, b in enumerate(self.t_bits))
            self.groups.append(
                [base | sum(((h >> (2 - i)) & 1) << b for i, b in enumerate(self.h_bits)) for h in range(8)]
            )

    def swapped(self, device):
        return sum(((device >> b) & 1) << self.swap[b] for b in range(self.bits))

    def axis(self, bit):
        return self.bits - 1 - bit

    def flip(self, value, bit):
        return lax.ppermute(value, AXIS, [(d, d ^ (1 << bit)) for d in range(self.count)])

    def exchange_heads(self, value):
        return lax.ppermute(value, AXIS, [(d, self.swapped(d)) for d in range(self.count)])

    def mine(self, bit):
        return (lax.axis_index(AXIS) >> bit) & 1

    def gather(self, value):
        pieces = {0: value}
        for bit in self.t_bits:
            pieces.update({key | (1 << bit): self.flip(piece, bit) for key, piece in list(pieces.items())})
        return pieces

    def place(self, pieces, order, shape):
        some = pieces[0]
        whole = jnp.zeros(shape, some.dtype)
        block = tuple(1 if bit is not None else size for bit, size in zip(order, shape))
        block = block + shape[len(order) :]
        for key, piece in pieces.items():
            starts = [0 if bit is None else self.mine(bit) ^ ((key >> bit) & 1) for bit in order]
            starts = starts + [0] * (len(shape) - len(order))
            whole = lax.dynamic_update_slice(whole, piece.reshape(block), starts)
        return whole

    def reduce(self, part, order):
        order = list(order)
        for bit in reversed(self.t_bits):
            axis = order.index(bit)
            mine = self.mine(bit)
            away = lax.dynamic_index_in_dim(part, 1 - mine, axis, keepdims=False).astype(BF16)
            keep = lax.dynamic_index_in_dim(part, mine, axis, keepdims=False)
            part = keep + self.flip(away, bit).astype(F32)
            order.pop(axis)
        return part

    def gather_tokens(self, value):
        pieces = [value]
        for bit in self.h_bits[:-1]:
            pieces = pieces + [self.flip(piece, bit) for piece in pieces]
        own = jnp.concatenate(pieces, axis=0)
        return jnp.concatenate([own, self.flip(own, self.h_bits[-1])], axis=0)

    def reduce_tokens(self, part):
        for bit in reversed(self.h_bits):
            half = part.shape[0] // 2
            away = part[half:].astype(BF16)
            part = part[:half].astype(F32) + self.flip(away, bit).astype(F32)
        return part

    def to_columns(self, value):
        return lax.all_to_all(value, AXIS, split_axis=0, concat_axis=0, tiled=True, axis_index_groups=self.groups)


def local(
    inputs,
    doc_ids,
    attn_gain,
    attn_shift,
    ffn_gain,
    ffn_shift,
    qkv_weight,
    qkv_bias,
    proj_weight,
    proj_bias,
    up_weight,
    up_bias,
    down_weight,
    down_bias,
    cotangent,
):
    n = lax.axis_size(AXIS)
    lay = Layout(n)
    bits = lay.bits
    two = (2,) * bits
    count, width = inputs.shape
    rows = width // n
    unit = up_bias.shape[0]
    hidden = unit * (n // HEADS)
    h_axes = [lay.axis(b) for b in lay.h_bits]
    t_axes = [lay.axis(b) for b in lay.t_bits]

    small = jnp.concatenate(
        [
            attn_gain,
            attn_shift,
            ffn_gain,
            ffn_shift,
            proj_bias,
            down_bias,
            qkv_bias,
            up_bias,
            doc_ids[0].astype(BF16),
        ]
    )
    small = lax.all_to_all(
        jnp.broadcast_to(small[None], (n, small.shape[0])), AXIS, split_axis=0, concat_axis=0, tiled=True
    ).astype(F32)
    sizes = [rows] * 6 + [3 * rows, unit, count]
    vectors, at = [], 0
    for size in sizes:
        vectors.append(small[:, at : at + size])
        at += size
    a_gain, a_shift, f_gain, f_shift, b_proj, b_down = [v.reshape(1, width) for v in vectors[:6]]

    heads_at = [2 + (bits - 1 - lay.swap[b]) for b in lay.h_bits]
    up_cols = up_weight.reshape((rows,) + two + (unit,))
    up_cols = up_cols.transpose([1 + a for a in h_axes] + [0] + [1 + a for a in t_axes] + [bits + 1])
    up_cols = lay.to_columns(up_cols.reshape(HEADS, rows, hidden))
    qkv_cols = qkv_weight.reshape(rows, 3, 2, 2, 2, HEAD).transpose(heads_at + [0, 1, 5])
    qkv_cols = lay.to_columns(qkv_cols.reshape(HEADS, rows, 3 * HEAD))

    x = lay.gather_tokens(inputs)
    row_order = [b if b in lay.t_bits else None for b in range(bits - 1, -1, -1)]
    w_up = lay.place(lay.gather(up_cols), row_order, two + (rows, hidden)).reshape(width, hidden)
    g = lay.gather_tokens(cotangent)
    t_two = (2,) * len(lay.t_bits)
    w_down = lay.place(lay.gather(down_weight), lay.t_bits, t_two + (unit, width)).reshape(hidden, width)
    proj_order = [lay.swap[b] for b in range(bits - 4, -1, -1)]
    w_proj = lay.place(
        lay.gather(lay.exchange_heads(proj_weight)), proj_order, t_two + (rows, width)
    ).reshape(HEAD, width)
    w_qkv = lay.place(lay.gather(qkv_cols), row_order, two + (rows, 3 * HEAD)).reshape(width, 3 * HEAD)

    b_up = vectors[7].reshape(two + (unit,)).transpose(h_axes + t_axes + [bits]).reshape(HEADS, hidden)
    b_qkv = vectors[6].reshape((3, 2, 2, 2, HEAD)).transpose([a - 1 for a in heads_at] + [0, 4]).reshape(HEADS, 3 * HEAD)
    here = sum(lay.mine(b) << (2 - i) for i, b in enumerate(lay.h_bits))
    b_up = lax.dynamic_index_in_dim(b_up, here, 0, keepdims=True)
    b_qkv = lax.dynamic_index_in_dim(b_qkv, here, 0, keepdims=True)
    me = lax.axis_index(AXIS)
    docs = []
    for j in range(HEADS):
        other = me ^ sum(((j >> i) & 1) << b for i, b in enumerate(lay.h_bits))
        docs.append(lax.dynamic_index_in_dim(vectors[8], other, 0, keepdims=True))
    docs = jnp.concatenate(docs, axis=0).astype(jnp.int32)

    index = jnp.arange(count, dtype=jnp.int32)
    same = docs[:, :, None] == docs[:, None, :]
    position = jnp.sum((same & (index[None, None, :] < index[None, :, None])).astype(jnp.int32), axis=2).reshape(-1)
    freq = 10000.0 ** (-2.0 * jnp.arange(ROT // 2, dtype=F32) / ROT)
    angle = position.astype(F32)[:, None] * freq[None, :]
    cosine, sine = jnp.cos(angle), jnp.sin(angle)
    rest = 128 - ROT
    cosine = jnp.concatenate([cosine, cosine, jnp.ones((angle.shape[0], rest), F32)], axis=1)
    sine = jnp.concatenate([-sine, sine, jnp.zeros((angle.shape[0], rest), F32)], axis=1)

    value = x.astype(F32)
    center = value - jnp.mean(value, axis=-1, keepdims=True)
    scale = lax.rsqrt(jnp.mean(center * center, axis=-1, keepdims=True) + EPS)
    xhat = center * scale
    first = (xhat * a_gain + a_shift).astype(BF16)
    second = (xhat * f_gain + f_shift).astype(BF16)

    up = jnp.dot(second, w_up, preferred_element_type=F32) + b_up
    phi_sum = 0.5 * (1.0 + lax.erf(up * (0.5**0.5)))
    act = (up * phi_sum).astype(BF16)
    slope = phi_sum + up * jnp.exp(-0.5 * up * up) * 0.3989422804014327
    part_down = times_tokens(act, g)
    d_act = times_rows(g, w_down)
    d_up = (d_act * slope).astype(BF16)
    part_up = times_tokens(second, d_up)
    d_second = times_rows(d_up, w_up)

    d_mixed = times_rows(g, w_proj).astype(BF16)
    qkv = jnp.dot(first, w_qkv, preferred_element_type=F32) + b_qkv
    mixed, d_qkv, column_qkv = attention(qkv, cosine, sine, docs, d_mixed)
    part_proj = times_tokens(mixed, g)
    part_qkv = times_tokens(first, d_qkv)
    d_first = times_rows(d_qkv, w_qkv)

    branches = jnp.dot(act, w_down, preferred_element_type=F32) + jnp.dot(mixed, w_proj, preferred_element_type=F32)
    value_own = inputs.astype(F32)
    layer_out = lay.reduce_tokens(branches) + value_own + b_proj + b_down

    edge = lay.reduce_tokens(d_first * a_gain + d_second * f_gain)
    center_own = value_own - jnp.mean(value_own, axis=-1, keepdims=True)
    scale_own = lax.rsqrt(jnp.mean(center_own * center_own, axis=-1, keepdims=True) + EPS)
    xhat_own = center_own * scale_own
    back = edge - jnp.mean(edge, axis=-1, keepdims=True) - xhat_own * jnp.mean(edge * xhat_own, axis=-1, keepdims=True)
    grad_inputs = cotangent.astype(F32) + back * scale_own

    grad_down = lay.reduce(part_down.reshape(t_two + (unit, width)), lay.t_bits)
    grad_proj = lay.reduce(part_proj.reshape(t_two + (rows, width)), proj_order)
    grad_proj = lay.exchange_heads(grad_proj.astype(BF16)).astype(F32)
    grad_up = lay.reduce(part_up.reshape(two + (rows, hidden)), row_order).reshape(HEADS, rows, hidden)
    grad_up = lay.to_columns(grad_up.astype(BF16)).astype(F32)
    axes = h_axes + t_axes
    grad_up = grad_up.reshape((2, 2, 2, rows) + t_two + (unit,))
    back_axes = [3] + [
        (axes.index(a) if axes.index(a) < 3 else axes.index(a) + 1) for a in range(bits)
    ] + [bits + 1]
    grad_up = grad_up.transpose(back_axes).reshape(rows, -1)
    grad_qkv = lay.reduce(part_qkv.reshape(two + (rows, 3 * HEAD)), row_order).reshape(HEADS, rows, 3 * HEAD)
    grad_qkv = lay.to_columns(grad_qkv.astype(BF16)).astype(F32)
    grad_qkv = grad_qkv.reshape(2, 2, 2, rows, 3, HEAD)
    grad_qkv = grad_qkv.transpose([3, 4] + [heads_at.index(a) for a in (2, 3, 4)] + [5]).reshape(rows, -1)

    column_up = jnp.sum(d_up.astype(F32), axis=0)
    column_out = jnp.sum(cotangent.astype(F32), axis=0)
    spread_up = lax.dynamic_update_slice(jnp.zeros((HEADS, hidden), F32), column_up[None], (here, 0))
    spread_up = spread_up.reshape((2,) * bits + (unit,)).transpose(
        [(axes.index(a)) for a in range(bits)] + [bits]
    )
    spread_qkv = lax.dynamic_update_slice(jnp.zeros((HEADS, 3 * HEAD), F32), column_qkv, (here, 0))
    spread_qkv = spread_qkv.reshape(2, 2, 2, 3, HEAD).transpose([3] + [heads_at.index(a) for a in (2, 3, 4)] + [4])
    sums = [
        jnp.sum(d_first * xhat, axis=0),
        jnp.sum(d_first, axis=0),
        jnp.sum(d_second * xhat, axis=0),
        jnp.sum(d_second, axis=0),
        column_out,
        spread_qkv,
        spread_up,
    ]
    sums = jnp.concatenate([s.reshape(n, -1) for s in sums], axis=1)
    sums = jnp.sum(lax.all_to_all(sums, AXIS, split_axis=0, concat_axis=0, tiled=True), axis=0)
    got, at = [], 0
    for size in [rows] * 5 + [3 * rows, unit]:
        got.append(sums[at : at + size])
        at += size
    return (
        layer_out,
        grad_inputs,
        got[0],
        got[1],
        got[2],
        got[3],
        grad_qkv,
        got[5],
        grad_proj,
        got[4],
        grad_up,
        got[6],
        grad_down,
        got[4],
    )


def solution(mesh):
    tokens, rows = P(AXIS, None), P(AXIS)
    return jax.shard_map(
        local,
        mesh=mesh,
        in_specs=(tokens, tokens, rows, rows, rows, rows, tokens, rows, tokens, rows, tokens, rows, tokens, rows, tokens),
        out_specs=(tokens, tokens, rows, rows, rows, rows, tokens, rows, tokens, rows, tokens, rows, tokens, rows),
        check_vma=False,
    )
```

time: 3430 us -> 684 us (0.20)
  waiting for transfers between devices: 2740 us -> 223 us
  starting transfers between devices: 0.28 us -> 105 us
  other arithmetic: 163 us -> 72.9 us
  matrix products: 231 us -> 147 us
  blocking collectives: 83.7 us -> 0 us
  local copies, waits for them, and re-layouts: 182 us -> 119 us
    unnamed x9 -> x0, waiting for transfers between devices: 1480 us -> none
    reduce_scatter x1 -> x0, waiting for transfers between devices: 872 us -> none  [local(): lax.psum_scatter(jnp.concatenate([part_proj, part_down], axis=1), 'fsdp',...]
    all_gather x4 -> x0, waiting for transfers between devices: 390 us -> none  [the longest x1 140 us: local(): lax.all_gather(up_weight, 'fsdp', axis=0, tiled=True)]
    ppermute x0 -> x36, waiting for transfers between devices: none -> 215 us  [the longest x34 215 us: flip(): lax.ppermute(value, AXIS, [(d, d ^ 1 << bit) for d in range(self.count)])]
    concatenate x2, other arithmetic: 133 us -> 5.95 us  [gather_tokens(): own = jnp.concatenate(pieces, axis=0)]
    reshape x5 -> x26, local copies, waits for them, and re-layouts: 141 us -> 24.7 us  [the longest x3 8.94 us: local(): grad_up = grad_up.transpose(back_axes).reshape(rows, -1)]
    dot_general x17 -> x12, matrix products: 225 us -> 147 us  [the longest x4 58.8 us: times_rows(): return jnp.einsum('tc,nc->tn', left, right, preferred_element_type=F32)]
    all_to_all x0 -> x6, starting transfers between devices: none -> 54.3 us  [the longest x4 45.9 us: to_columns(): lax.all_to_all(value, AXIS, split_axis=0, concat_axis=0, tiled=True, axis...]
  transfers between devices with their start and end apart: 7 -> 42, of which waited for: 5 -> 15; matrix products, arithmetic and copies ran while one was open for 13% -> 41% of each run, Pallas kernels for 0% -> 0%
where the time goes in v1:
time: 684 us; the launch traced here: 678 us
  waiting for transfers between devices  223 us (33%)
  matrix products  147 us (21%)
  local copies, waits for them, and re-layouts  119 us (17%)
  starting transfers between devices  105 us (15%)
  other arithmetic  72.9 us (11%)
  Pallas kernels  9.87 us (1%)
    ppermute x34, waiting for transfers between devices, flip(): lax.ppermute(value, AXIS, [(d, d ^ 1 << bit) for d in range(self.count)])  215 us
    dot_general x4, matrix products, times_rows(): return jnp.einsum('tc,nc->tn', left, right, preferred_element_type=F32)  58.8 us
    ppermute x34, starting transfers between devices, flip(): lax.ppermute(value, AXIS, [(d, d ^ 1 << bit) for d in range(self.count)])  48.1 us
    all_to_all x4, starting transfers between devices, to_columns(): lax.all_to_all(value, AXIS, split_axis=0, concat_axis=0, tiled=True, axis...  45.9 us
    dot_general x4, matrix products, times_tokens(): return jnp.einsum('tn,td->nd', left, right, preferred_element_type=F32)  45.5 us
    unnamed x100, local copies, waits for them, and re-layouts  27.2 us
    add x4, other arithmetic, reduce_tokens(): part = part[:half].astype(F32) + self.flip(away, bit).astype(F32)  21.9 us
    slice x6, local copies, waits for them, and re-layouts, reduce_tokens(): away = part[half:].astype(BF16)  17.6 us
  transfers between devices with their start and end apart: 42, of which 15 were waited for; matrix products, arithmetic and copies ran while one was open for 41% of the time, Pallas kernels for 0%

profile of v1, /device:TPU:0, one launch (start us, length us, event | category | flops | bytes accessed | tf_op | source)
XLA Modules:
  0.0 678.1 jit_solution(5480364363164140944)
XLA Ops:
  6.0 5.4 concatenate.83
  58.1 31.3 %collective-permute-done.18 = bf16[64,2048]{1,0:T(8,128)(2,1)S(1)} collective-permute-done((bf16[64,2048]{1,0:T(8,128)(2,1)S(1)}, bf16[64,2048]{1,0:T(8,128)(2,1)S(1)}, u32[]{:S(2)}, u32[]{:S(2)}) %collective-permute-start.18) | collective-permute-done | bytes 262176 | tf_op jit(solution)/shard_map/ppermute | solution.py:133
  92.1 6.0 collective-permute-done.19
  100.4 6.6 collective-permute-done.20
  109.7 7.8 %all-to-all-start.1 = ((bf16[8,64,1024]{2,1,0:T(8,128)(2,1)}), bf16[8,64,1024]{2,1,0:T(8,128)(2,1)}, u32[]{:S(2)}, u32[]{:S(2)}) async-start(bf16[8,64,1024]{2,1,0:T(8,128)(2,1)} %reshape.512), calls=%async_computation.1 | async-start | bytes 2097152 | tf_op jit(solution)/shard_map/all_to_all | solution.py:184
  128.4 5.0 collective-permute-done.8
  138.1 7.0 %collective-permute-done.14 = bf16[256,2048]{1,0:T(8,128)(2,1)} collective-permute-done((bf16[256,2048]{1,0:T(8,128)(2,1)}, bf16[256,2048]{1,0:T(8,128)(2,1)}, u32[]{:S(2)}, u32[]{:S(2)}) %collective-permute-start.14) | collective-permute-done | bytes 1048608 | tf_op jit(solution)/shard_map/ppermute | solution.py:133
  154.3 18.9 %collective-permute-done.15 = bf16[256,2048]{1,0:T(8,128)(2,1)} collective-permute-done((bf16[256,2048]{1,0:T(8,128)(2,1)}, bf16[256,2048]{1,0:T(8,128)(2,1)}, u32[]{:S(2)}, u32[]{:S(2)}) %collective-permute-start.15) | collective-permute-done | bytes 1048608 | tf_op jit(solution)/shard_map/ppermute | solution.py:133
  186.9 31.0 %collective-permute-done.4 = bf16[8,64,1024]{2,1,0:T(8,128)(2,1)S(1)} collective-permute-done((bf16[8,64,1024]{2,1,0:T(8,128)(2,1)}, bf16[8,64,1024]{2,1,0:T(8,128)(2,1)S(1)}, u32[]{:S(2)}, u32[]{:S(2)}) %collective-permute-start.4) | collective-permute-done | bytes 1048608 | tf_op jit(solution)/shard_map/ppermute | solution.py:133
  220.8 11.2 %collective-permute-done.10 = bf16[8,64,768]{2,1,0:T(8,128)(2,1)S(1)} collective-permute-done((bf16[8,64,768]{2,1,0:T(8,128)(2,1)}, bf16[8,64,768]{2,1,0:T(8,128)(2,1)S(1)}, u32[]{:S(2)}, u32[]{:S(2)}) %collective-permute-start.10) | collective-permute-done | bytes 786464 | tf_op jit(solution)/shard_map/ppermute | solution.py:133
  234.2 20.2 %collective-permute-done.12 = bf16[8,64,768]{2,1,0:T(8,128)(2,1)S(1)} collective-permute-done((bf16[8,64,768]{2,1,0:T(8,128)(2,1)S(1)}, bf16[8,64,768]{2,1,0:T(8,128)(2,1)S(1)}, u32[]{:S(2)}, u32[]{:S(2)}) %collective-permute-start.12) | collective-permute-done | bytes 786464 | tf_op jit(solution)/shard_map/ppermute | solution.py:133
  268.9 6.0 convolution_convert_fusion.d_mixed_ref
  279.0 6.8 %broadcast_add_fusion.qkv_ref = f32[2048,768]{1,0:T(8,128)S(1)} fusion(f32[768]{0:T(1024)S(1)} %fusion.42, bf16[2048,2048]{1,0:T(8,128)(2,1)S(1)} %fusion.9, bf16[2048,768]{1,0:T(8,128)(2,1)S(1)} %bitcast.186), kind=kOutput, calls=%fused_computation.46 | convolution fusion | flops 6444023808 | bytes 17828864 | tf_op jit(solution)/shard_map/dot_general | solution.py:297
  285.9 9.9 %shard_map.254 = (bf16[2048,256]{1,0:T(8,128)(2,1)S(1)}, bf16[2048,768]{1,0:T(8,128)(2,1)S(1)}, f32[1,768]{1,0:T(1,128)S(1)}) custom-call(f32[2048,768]{1,0:T(8,128)S(1)} %broadcast_add_fusion.qkv_ref, f32[2,2048,128]{2,1,0:T(8,128)S(1)} %pad_maximum_fusion.2.turn_ref, s32[8,1,256]{2,1,0:T(1,128)S(1)} %convert_element_type.204.docs_row_ref, ...), custom_call_target="tpu_custom_call" | custom-call | flops 2147483648 | bytes 10485760 | tf_op jit(solution)/shard_map/pallas_call | solution.py:74
  295.8 11.1 %fusion.54 = f32[2048,768]{1,0:T(8,128)} fusion(bf16[2048,2048]{1,0:T(8,128)(2,1)} %copy-done.14, bf16[2048,768]{1,0:T(8,128)(2,1)S(1)} %get-tuple-element.18), kind=kOutput, calls=%fused_computation.169 | convolution fusion | flops 6442450944 | bytes 17825792 | tf_op jit(solution)/shard_map/tn,td->nd/dot_general | solution.py:106
  306.9 9.7 %fusion.53 = f32[2048,2048]{1,0:T(8,128)} fusion(bf16[2048,768]{1,0:T(8,128)(2,1)S(1)} %get-tuple-element.18, bf16[2048,768]{1,0:T(8,128)(2,1)S(1)} %bitcast.187), kind=kOutput, calls=%fused_computation.168 | convolution fusion | flops 6442450944 | bytes 23068672 | tf_op jit(solution)/shard_map/tc,nc->tn/dot_general | solution.py:102
  325.3 12.4 %multiply_convert_fusion = (bf16[2048,1024]{1,0:T(8,128)(2,1)S(1)}, f32[2048,1024]{1,0:T(8,128)}) fusion(f32[1024]{0:T(1024)S(1)} %bitcast.212, bf16[2048,1024]{1,0:T(8,128)(2,1)S(1)} %bitcast.182, bf16[2048,2048]{1,0:T(8,128)(2,1)S(1)} %constant_dynamic-update-slice_fusion, f32[2048]{0:T(1024)S(1)} %add.256, f32[2048]{0:T(1024)S(1)} %mul.132, ...), kind=kOutput, calls=%fused_computation.29 | convolution fusion | flops 8627683328 | bytes 25202688 | tf_op jit(solution)/shard_map/dot_general | solution.py:286
  337.7 19.2 %convert_reduce_fusion.1 = (f32[1024]{0:T(1024)S(1)}, bf16[2048,1024]{1,0:T(8,128)(2,1)}) fusion(f32[2048,1024]{1,0:T(8,128)} %get-tuple-element.65, f32[1024]{0:T(1024)S(1)} %bitcast.213, bf16[2048,2048]{1,0:T(8,128)(2,1)} %constant_dynamic-update-slice_fusion.21, bf16[1024,2048]{1,0:T(8,128)(2,1)} %bitcast.16), kind=kOutput, calls=%fused_computation.28 | convolution fusion | flops 8617196544 | bytes 25174016 | tf_op jit(solution)/shard_map/tc,nc->tn/dot_general | solution.py:102
  356.9 13.2 %fusion.43 = f32[2048,1024]{1,0:T(8,128)S(1)} fusion(bf16[2048,1024]{1,0:T(8,128)(2,1)} %get-tuple-element.67, bf16[2048,2048]{1,0:T(8,128)(2,1)S(1)} %constant_dynamic-update-slice_fusion, f32[2048]{0:T(1024)S(1)} %add.256, f32[2048]{0:T(1024)S(1)} %mul.132, f32[2048]{0:T(1024)S(1)} %add_rsqrt_fusion, f32[2048]{0:T(1024)S(1)} %broadcast_multiply_fusion), kind=kOutput, calls=%fused_computation.160 | convolution fusion | flops 8615100416 | bytes 21004288 | tf_op jit(solution)/shard_map/tn,td->nd/dot_general | solution.py:106
  375.6 14.5 %fusion.52 = f32[2048,2048]{1,0:T(8,128)} fusion(bf16[2048,1024]{1,0:T(8,128)(2,1)S(1)} %get-tuple-element.64, bf16[1024,2048]{1,0:T(8,128)(2,1)} %bitcast.16), kind=kOutput, calls=%fused_computation.167 | convolution fusion | flops 8589934592 | bytes 25165824 | tf_op jit(solution)/shard_map/dot_general | solution.py:303
  390.1 23.9 %fusion.47 = (f32[2048]{0:T(1024)S(1)}, f32[2048]{0:T(1024)S(1)}, f32[2048,2048]{1,0:T(8,128)}, f32[2048]{0:T(1024)S(1)}, f32[2048]{0:T(1024)S(1)}) fusion(f32[2048]{0:T(1024)S(1)} %add_rsqrt_fusion, f32[2048]{0:T(1024)S(1)} %broadcast_multiply_fusion, bf16[2048,2048]{1,0:T(8,128)(2,1)} %copy-done.3, f32[2048]{0:T(1024)S(1)} %mul.132, ...), kind=kOutput, calls=%fused_computation.162 | convolution fusion | flops 8640258048 | bytes 50397184 | tf_op jit(solution)/shard_map/tc,nc->tn/dot_general | solution.py:102
  414.0 6.0 slice.159
  420.0 8.5 %convolution_add_fusion = f32[2048,2048]{1,0:T(8,128)S(1)} fusion(f32[2048,2048]{1,0:T(8,128)} %fusion.52, bf16[2048,256]{1,0:T(8,128)(2,1)S(1)} %get-tuple-element.17, bf16[256,2048]{1,0:T(8,128)(2,1)} %bitcast.50), kind=kOutput, calls=%fused_computation.17 | convolution fusion | flops 2151677952 | bytes 35651584 | tf_op jit(solution)/shard_map/dot_general | solution.py:303
  432.4 18.8 %fusion.56 = f32[1024,2048]{1,0:T(8,128)} fusion(bf16[2048,1024]{1,0:T(8,128)(2,1)} %copy-done.31, bf16[2048,2048]{1,0:T(8,128)(2,1)} %constant_dynamic-update-slice_fusion.21), kind=kOutput, calls=%fused_computation.171 | convolution fusion | flops 8589934592 | bytes 20971520 | tf_op jit(solution)/shard_map/tn,td->nd/dot_general | solution.py:106
  464.0 5.8 slice_add_fusion
  474.2 9.9 %slice_add_fusion.1 = f32[1024,2048]{1,0:T(8,128)} fusion(f32[2048,2048]{1,0:T(8,128)} %copy-done.1, bf16[1024,2048]{1,0:T(8,128)(2,1)} %collective-permute-done.21), kind=kLoop, calls=%fused_computation.27 | loop fusion | flops 4194304 | bytes 20971520 | tf_op jit(solution)/shard_map/add | solution.py:180
  489.7 17.9 %collective-permute-done.30 = bf16[64,2048]{1,0:T(8,128)(2,1)S(1)} collective-permute-done((bf16[64,2048]{1,0:T(8,128)(2,1)S(1)}, bf16[64,2048]{1,0:T(8,128)(2,1)S(1)}, u32[]{:S(2)}, u32[]{:S(2)}) %collective-permute-start.30) | collective-permute-done | bytes 262176 | tf_op jit(solution)/shard_map/ppermute | solution.py:133
  515.3 12.0 %collective-permute-done.28 = bf16[2,2,2,64,768]{4,3,2,1,0:T(8,128)(2,1)} collective-permute-done((bf16[2,2,2,64,768]{4,3,2,1,0:T(8,128)(2,1)S(1)}, bf16[2,2,2,64,768]{4,3,2,1,0:T(8,128)(2,1)}, u32[]{:S(2)}, u32[]{:S(2)}) %collective-permute-start.28) | collective-permute-done | bytes 786464 | tf_op jit(solution)/shard_map/ppermute | solution.py:133
  530.1 30.1 %all-to-all-start.4 = ((bf16[8,64,768]{2,1,0:T(8,128)(2,1)}), bf16[8,64,768]{2,1,0:T(8,128)(2,1)S(1)}, u32[]{:S(2)}, u32[]{:S(2)}) async-start(bf16[8,64,768]{2,1,0:T(8,128)(2,1)} %bitcast.60), calls=%async_computation.4 | async-start | bytes 1572864 | tf_op jit(solution)/shard_map/all_to_all | solution.py:184
  591.1 25.9 %collective-permute-done.26 = bf16[256,2048]{1,0:T(8,128)(2,1)S(1)} collective-permute-done((bf16[256,2048]{1,0:T(8,128)(2,1)}, bf16[256,2048]{1,0:T(8,128)(2,1)S(1)}, u32[]{:S(2)}, u32[]{:S(2)}) %collective-permute-start.26) | collective-permute-done | bytes 1048608 | tf_op jit(solution)/shard_map/ppermute | solution.py:133
  617.7 21.8 %collective-permute-done.23 = bf16[256,2048]{1,0:T(8,128)(2,1)} collective-permute-done((bf16[256,2048]{1,0:T(8,128)(2,1)}, bf16[256,2048]{1,0:T(8,128)(2,1)}, u32[]{:S(2)}, u32[]{:S(2)}) %collective-permute-start.23) | collective-permute-done | bytes 1048608 | tf_op jit(solution)/shard_map/ppermute | solution.py:133
  639.6 5.2 convert_reduce_fusion.3
  (310 shorter events, 236.6 us)
Async XLA Ops:
  0.7 117.5 %collective-permute-start.1 = (bf16[256,2048]{1,0:T(8,128)(2,1)}, bf16[256,2048]{1,0:T(8,128)(2,1)}, u32[]{:S(2)}, u32[]{:S(2)}) collective-permute-start(bf16[256,2048]{1,0:T(8,128)(2,1)} %param.15), channel_id=1, source_target_pairs={{0,4},{1,5},{2,6},{3,7},{4,0},{5,1},{6,2},{7,3},{8,12},{9,13},{10,... | collective-permute-start | bytes 3145736 | tf_op jit(solution)/shard_map/ppermute | solution.py:133
  3.7 87.2 %collective-permute-start = (bf16[256,2048]{1,0:T(8,128)(2,1)}, bf16[256,2048]{1,0:T(8,128)(2,1)}, u32[]{:S(2)}, u32[]{:S(2)}) collective-permute-start(bf16[256,2048]{1,0:T(8,128)(2,1)} %param.15), channel_id=1, source_target_pairs={{0,8},{1,9},{2,10},{3,11},{4,12},{5,13},{6,14},{7,15},{8,0},{9,1},... | collective-permute-start | bytes 3145736 | tf_op jit(solution)/shard_map/ppermute | solution.py:133
  17.7 38.1 %collective-permute-start.17 = (bf16[64,2048]{1,0:T(8,128)(2,1)}, bf16[64,2048]{1,0:T(8,128)(2,1)S(1)}, u32[]{:S(2)}, u32[]{:S(2)}) collective-permute-start(bf16[64,2048]{1,0:T(8,128)(2,1)} %param.23), channel_id=1, source_target_pairs={{0,0},{1,16},{2,2},{3,18},{4,4},{5,20},{6,6},{7,22},{8,8},{9,24},{... | collective-permute-start | bytes 786440 | tf_op jit(solution)/shard_map/ppermute | solution.py:136
  19.3 89.9 %collective-permute-start.7 = (bf16[256,2048]{1,0:T(8,128)(2,1)}, bf16[256,2048]{1,0:T(8,128)(2,1)}, u32[]{:S(2)}, u32[]{:S(2)}) collective-permute-start(bf16[256,2048]{1,0:T(8,128)(2,1)} %param.27), channel_id=1, source_target_pairs={{0,16},{1,17},{2,18},{3,19},{4,20},{5,21},{6,22},{7,23},{8,24},{9,... | collective-permute-start | bytes 3145736 | tf_op jit(solution)/shard_map/ppermute | solution.py:133
  22.5 95.1 %collective-permute-start.13 = (bf16[256,2048]{1,0:T(8,128)(2,1)}, bf16[256,2048]{1,0:T(8,128)(2,1)}, u32[]{:S(2)}, u32[]{:S(2)}) collective-permute-start(bf16[256,2048]{1,0:T(8,128)(2,1)} %param.29), channel_id=1, source_target_pairs={{0,8},{1,9},{2,10},{3,11},{4,12},{5,13},{6,14},{7,15},{8,0},{9,1},... | collective-permute-start | bytes 3145736 | tf_op jit(solution)/shard_map/ppermute | solution.py:133
  42.1 67.6 %all-to-all-start.2 = ((bf16[8,64,768]{2,1,0:T(8,128)(2,1)}), bf16[8,64,768]{2,1,0:T(8,128)(2,1)}, u32[]{:S(2)}, u32[]{:S(2)}) async-start(bf16[8,64,768]{2,1,0:T(8,128)(2,1)} %reshape.526), calls=%async_computation.2 | async-start | bytes 1572864 | tf_op jit(solution)/shard_map/all_to_all | solution.py:184
  109.7 41.4 %all-to-all-start.1 = ((bf16[8,64,1024]{2,1,0:T(8,128)(2,1)}), bf16[8,64,1024]{2,1,0:T(8,128)(2,1)}, u32[]{:S(2)}, u32[]{:S(2)}) async-start(bf16[8,64,1024]{2,1,0:T(8,128)(2,1)} %reshape.512), calls=%async_computation.1 | async-start | bytes 2097152 | tf_op jit(solution)/shard_map/all_to_all | solution.py:184
  117.6 61.2 %collective-permute-start.9 = (bf16[256,2048]{1,0:T(8,128)(2,1)}, bf16[256,2048]{1,0:T(8,128)(2,1)}, u32[]{:S(2)}, u32[]{:S(2)}) collective-permute-start(bf16[256,2048]{1,0:T(8,128)(2,1)} %collective-permute-done.7), channel_id=1, source_target_pairs={{0,2},{1,3},{2,0},{3,1},{4,6},{5,7},{6,4},{7,5},{8,10},{9,11},{10,... | collective-permute-start | bytes 3145736 | tf_op jit(solution)/shard_map/ppermute | solution.py:133
  118.2 55.0 %collective-permute-start.15 = (bf16[256,2048]{1,0:T(8,128)(2,1)}, bf16[256,2048]{1,0:T(8,128)(2,1)}, u32[]{:S(2)}, u32[]{:S(2)}) collective-permute-start(bf16[256,2048]{1,0:T(8,128)(2,1)} %collective-permute-done.13), channel_id=1, source_target_pairs={{0,4},{1,5},{2,6},{3,7},{4,0},{5,1},{6,2},{7,3},{8,12},{9,13},{10,... | collective-permute-start | bytes 3145736 | tf_op jit(solution)/shard_map/ppermute | solution.py:133
  123.8 134.3 %collective-permute-start.3 = (bf16[1024,2048]{1,0:T(8,128)(2,1)}, bf16[1024,2048]{1,0:T(8,128)(2,1)}, u32[]{:S(2)}, u32[]{:S(2)}) collective-permute-start(bf16[1024,2048]{1,0:T(8,128)(2,1)} %pad_maximum_fusion), channel_id=1, source_target_pairs={{0,1},{1,0},{2,3},{3,2},{4,5},{5,4},{6,7},{7,6},{8,9},{9,8},{10,11... | collective-permute-start | bytes 12582920 | tf_op jit(solution)/shard_map/ppermute | solution.py:133
  147.4 36.6 %collective-permute-start.11 = (bf16[8,64,768]{2,1,0:T(8,128)(2,1)}, bf16[8,64,768]{2,1,0:T(8,128)(2,1)S(1)}, u32[]{:S(2)}, u32[]{:S(2)}) collective-permute-start(bf16[8,64,768]{2,1,0:T(8,128)(2,1)} %all-to-all-done.2), channel_id=1, source_target_pairs={{0,2},{1,3},{2,0},{3,1},{4,6},{5,7},{6,4},{7,5},{8,10},{9,11},{10,... | collective-permute-start | bytes 2359304 | tf_op jit(solution)/shard_map/ppermute | solution.py:133
  151.1 66.8 %collective-permute-start.4 = (bf16[8,64,1024]{2,1,0:T(8,128)(2,1)}, bf16[8,64,1024]{2,1,0:T(8,128)(2,1)S(1)}, u32[]{:S(2)}, u32[]{:S(2)}) collective-permute-start(bf16[8,64,1024]{2,1,0:T(8,128)(2,1)} %all-to-all-done.1), channel_id=1, source_target_pairs={{0,16},{1,17},{2,18},{3,19},{4,20},{5,21},{6,22},{7,23},{8,24},{9,... | collective-permute-start | bytes 3145736 | tf_op jit(solution)/shard_map/ppermute | solution.py:133
  175.6 88.5 %collective-permute-start.16 = (bf16[1024,2048]{1,0:T(8,128)(2,1)S(1)}, bf16[1024,2048]{1,0:T(8,128)(2,1)}, u32[]{:S(2)}, u32[]{:S(2)}) collective-permute-start(bf16[1024,2048]{1,0:T(8,128)(2,1)S(1)} %pad_maximum_fusion.1), channel_id=1, source_target_pairs={{0,1},{1,0},{2,3},{3,2},{4,5},{5,4},{6,7},{7,6},{8,9},{9,8},{10,11... | collective-permute-start | bytes 12582920 | tf_op jit(solution)/shard_map/ppermute | solution.py:133
  178.7 53.2 %collective-permute-start.10 = (bf16[8,64,768]{2,1,0:T(8,128)(2,1)}, bf16[8,64,768]{2,1,0:T(8,128)(2,1)S(1)}, u32[]{:S(2)}, u32[]{:S(2)}) collective-permute-start(bf16[8,64,768]{2,1,0:T(8,128)(2,1)} %all-to-all-done.2), channel_id=1, source_target_pairs={{0,16},{1,17},{2,18},{3,19},{4,20},{5,21},{6,22},{7,23},{8,24},{9,... | collective-permute-start | bytes 2359304 | tf_op jit(solution)/shard_map/ppermute | solution.py:133
  184.0 50.1 %collective-permute-start.5 = (bf16[8,64,1024]{2,1,0:T(8,128)(2,1)}, bf16[8,64,1024]{2,1,0:T(8,128)(2,1)S(1)}, u32[]{:S(2)}, u32[]{:S(2)}) collective-permute-start(bf16[8,64,1024]{2,1,0:T(8,128)(2,1)} %all-to-all-done.1), channel_id=1, source_target_pairs={{0,2},{1,3},{2,0},{3,1},{4,6},{5,7},{6,4},{7,5},{8,10},{9,11},{10,... | collective-permute-start | bytes 3145736 | tf_op jit(solution)/shard_map/ppermute | solution.py:133
  217.9 36.5 %collective-permute-start.6 = (bf16[8,64,1024]{2,1,0:T(8,128)(2,1)S(1)}, bf16[8,64,1024]{2,1,0:T(8,128)(2,1)S(1)}, u32[]{:S(2)}, u32[]{:S(2)}) collective-permute-start(bf16[8,64,1024]{2,1,0:T(8,128)(2,1)S(1)} %collective-permute-done.4), channel_id=1, source_target_pairs={{0,2},{1,3},{2,0},{3,1},{4,6},{5,7},{6,4},{7,5},{8,10},{9,11},{10,... | collective-permute-start | bytes 3145736 | tf_op jit(solution)/shard_map/ppermute | solution.py:133
  319.9 132.7 %collective-permute-start.27 = (bf16[2,2,2,2,64,768]{5,4,3,2,1,0:T(8,128)(2,1)}, bf16[2,2,2,2,64,768]{5,4,3,2,1,0:T(8,128)(2,1)}, u32[]{:S(2)}, u32[]{:S(2)}) collective-permute-start(bf16[2,2,2,2,64,768]{5,4,3,2,1,0:T(8,128)(2,1)} %fusion.32), channel_id=1, source_target_pairs={{0,2},{1,3},{2,0},{3,1},{4,6},{5,7},{6,4},{7,5},{8,10},{9,11},{10,... | collective-permute-start | bytes 4718600 | tf_op jit(solution)/shard_map/ppermute | solution.py:133
  323.8 127.5 %collective-permute-start.29 = (bf16[2,64,2048]{2,1,0:T(8,128)(2,1)}, bf16[2,64,2048]{2,1,0:T(8,128)(2,1)}, u32[]{:S(2)}, u32[]{:S(2)}) collective-permute-start(bf16[2,64,2048]{2,1,0:T(8,128)(2,1)} %fusion.38), channel_id=1, source_target_pairs={{0,2},{1,3},{2,0},{3,1},{4,6},{5,7},{6,4},{7,5},{8,10},{9,11},{10,... | collective-permute-start | bytes 1572872 | tf_op jit(solution)/shard_map/ppermute | solution.py:133
  375.0 83.3 %collective-permute-start.32 = (bf16[2,2,2,2,64,1024]{5,4,3,2,1,0:T(8,128)(2,1)}, bf16[2,2,2,2,64,1024]{5,4,3,2,1,0:T(8,128)(2,1)}, u32[]{:S(2)}, u32[]{:S(2)}) collective-permute-start(bf16[2,2,2,2,64,1024]{5,4,3,2,1,0:T(8,128)(2,1)} %fusion.29), channel_id=1, source_target_pairs={{0,2},{1,3},{2,0},{3,1},{4,6},{5,7},{6,4},{7,5},{8,10},{9,11},{10,... | collective-permute-start | bytes 6291464 | tf_op jit(solution)/shard_map/ppermute | solution.py:133
  420.0 43.9 %collective-permute-start.24 = (bf16[1024,2048]{1,0:T(8,128)(2,1)}, bf16[1024,2048]{1,0:T(8,128)(2,1)}, u32[]{:S(2)}, u32[]{:S(2)}) collective-permute-start(bf16[1024,2048]{1,0:T(8,128)(2,1)} %slice.159), channel_id=1, source_target_pairs={{0,1},{1,0},{2,3},{3,2},{4,5},{5,4},{6,7},{7,6},{8,9},{9,8},{10,11... | collective-permute-start | bytes 12582920 | tf_op jit(solution)/shard_map/ppermute | solution.py:133
  431.9 42.3 %collective-permute-start.21 = (bf16[1024,2048]{1,0:T(8,128)(2,1)}, bf16[1024,2048]{1,0:T(8,128)(2,1)}, u32[]{:S(2)}, u32[]{:S(2)}) collective-permute-start(bf16[1024,2048]{1,0:T(8,128)(2,1)} %slice.160), channel_id=1, source_target_pairs={{0,1},{1,0},{2,3},{3,2},{4,5},{5,4},{6,7},{7,6},{8,9},{9,8},{10,11... | collective-permute-start | bytes 12582920 | tf_op jit(solution)/shard_map/ppermute | solution.py:133
  452.5 55.1 %collective-permute-start.30 = (bf16[64,2048]{1,0:T(8,128)(2,1)S(1)}, bf16[64,2048]{1,0:T(8,128)(2,1)S(1)}, u32[]{:S(2)}, u32[]{:S(2)}) collective-permute-start(bf16[64,2048]{1,0:T(8,128)(2,1)S(1)} %fusion.41), channel_id=1, source_target_pairs={{0,16},{1,17},{2,18},{3,19},{4,20},{5,21},{6,22},{7,23},{8,24},{9,... | collective-permute-start | bytes 786440 | tf_op jit(solution)/shard_map/ppermute | solution.py:133
  455.4 72.0 %collective-permute-start.28 = (bf16[2,2,2,64,768]{4,3,2,1,0:T(8,128)(2,1)S(1)}, bf16[2,2,2,64,768]{4,3,2,1,0:T(8,128)(2,1)}, u32[]{:S(2)}, u32[]{:S(2)}) collective-permute-start(bf16[2,2,2,64,768]{4,3,2,1,0:T(8,128)(2,1)S(1)} %fusion.36), channel_id=1, source_target_pairs={{0,16},{1,17},{2,18},{3,19},{4,20},{5,21},{6,22},{7,23},{8,24},{9,... | collective-permute-start | bytes 2359304 | tf_op jit(solution)/shard_map/ppermute | solution.py:133
  462.1 98.1 %collective-permute-start.33 = (bf16[2,2,2,64,1024]{4,3,2,1,0:T(8,128)(2,1)S(1)}, bf16[2,2,2,64,1024]{4,3,2,1,0:T(8,128)(2,1)S(1)}, u32[]{:S(2)}, u32[]{:S(2)}) collective-permute-start(bf16[2,2,2,64,1024]{4,3,2,1,0:T(8,128)(2,1)S(1)} %fusion.34), channel_id=1, source_target_pairs={{0,16},{1,17},{2,18},{3,19},{4,20},{5,21},{6,22},{7,23},{8,24},{9,... | collective-permute-start | bytes 3145736 | tf_op jit(solution)/shard_map/ppermute | solution.py:133
  471.7 91.6 %collective-permute-start.25 = (bf16[512,2048]{1,0:T(8,128)(2,1)}, bf16[512,2048]{1,0:T(8,128)(2,1)}, u32[]{:S(2)}, u32[]{:S(2)}) collective-permute-start(bf16[512,2048]{1,0:T(8,128)(2,1)} %slice.161), channel_id=1, source_target_pairs={{0,4},{1,5},{2,6},{3,7},{4,0},{5,1},{6,2},{7,3},{8,12},{9,13},{10,... | collective-permute-start | bytes 6291464 | tf_op jit(solution)/shard_map/ppermute | solution.py:133
  488.0 82.2 %collective-permute-start.22 = (bf16[512,2048]{1,0:T(8,128)(2,1)}, bf16[512,2048]{1,0:T(8,128)(2,1)}, u32[]{:S(2)}, u32[]{:S(2)}) collective-permute-start(bf16[512,2048]{1,0:T(8,128)(2,1)} %slice.162), channel_id=1, source_target_pairs={{0,4},{1,5},{2,6},{3,7},{4,0},{5,1},{6,2},{7,3},{8,12},{9,13},{10,... | collective-permute-start | bytes 6291464 | tf_op jit(solution)/shard_map/ppermute | solution.py:133
  512.2 70.7 %collective-permute-start.34 = (bf16[2,256,2048]{2,1,0:T(8,128)(2,1)}, bf16[2,256,2048]{2,1,0:T(8,128)(2,1)}, u32[]{:S(2)}, u32[]{:S(2)}) collective-permute-start(bf16[2,256,2048]{2,1,0:T(8,128)(2,1)} %fusion.30), channel_id=1, source_target_pairs={{0,2},{1,3},{2,0},{3,1},{4,6},{5,7},{6,4},{7,5},{8,10},{9,11},{10,... | collective-permute-start | bytes 6291464 | tf_op jit(solution)/shard_map/ppermute | solution.py:133
  530.1 49.2 %all-to-all-start.4 = ((bf16[8,64,768]{2,1,0:T(8,128)(2,1)}), bf16[8,64,768]{2,1,0:T(8,128)(2,1)S(1)}, u32[]{:S(2)}, u32[]{:S(2)}) async-start(bf16[8,64,768]{2,1,0:T(8,128)(2,1)} %bitcast.60), calls=%async_computation.4 | async-start | bytes 1572864 | tf_op jit(solution)/shard_map/all_to_all | solution.py:184
  568.2 48.8 %collective-permute-start.26 = (bf16[256,2048]{1,0:T(8,128)(2,1)}, bf16[256,2048]{1,0:T(8,128)(2,1)S(1)}, u32[]{:S(2)}, u32[]{:S(2)}) collective-permute-start(bf16[256,2048]{1,0:T(8,128)(2,1)} %slice.163), channel_id=1, source_target_pairs={{0,8},{1,9},{2,10},{3,11},{4,12},{5,13},{6,14},{7,15},{8,0},{9,1},... | collective-permute-start | bytes 3145736 | tf_op jit(solution)/shard_map/ppermute | solution.py:133
  575.1 64.5 %collective-permute-start.23 = (bf16[256,2048]{1,0:T(8,128)(2,1)}, bf16[256,2048]{1,0:T(8,128)(2,1)}, u32[]{:S(2)}, u32[]{:S(2)}) collective-permute-start(bf16[256,2048]{1,0:T(8,128)(2,1)} %slice.164), channel_id=1, source_target_pairs={{0,8},{1,9},{2,10},{3,11},{4,12},{5,13},{6,14},{7,15},{8,0},{9,1},... | collective-permute-start | bytes 3145736 | tf_op jit(solution)/shard_map/ppermute | solution.py:133
  579.3 71.2 %all-to-all-start.5 = ((bf16[8,64,1024]{2,1,0:T(8,128)(2,1)}), bf16[8,64,1024]{2,1,0:T(8,128)(2,1)S(1)}, u32[]{:S(2)}, u32[]{:S(2)}) async-start(bf16[8,64,1024]{2,1,0:T(8,128)(2,1)} %bitcast.72), calls=%async_computation.5 | async-start | bytes 2097152 | tf_op jit(solution)/shard_map/all_to_all | solution.py:184
  589.7 65.3 %collective-permute-start.35 = (bf16[256,2048]{1,0:T(8,128)(2,1)}, bf16[256,2048]{1,0:T(8,128)(2,1)S(1)}, u32[]{:S(2)}, u32[]{:S(2)}) collective-permute-start(bf16[256,2048]{1,0:T(8,128)(2,1)} %fusion.35), channel_id=1, source_target_pairs={{0,16},{1,17},{2,18},{3,19},{4,20},{5,21},{6,22},{7,23},{8,24},{9,... | collective-permute-start | bytes 3145736 | tf_op jit(solution)/shard_map/ppermute | solution.py:133
  (46 other events, 853.9 us)
